TPU v7x, 512 devices: a whole 4x4x16 slice. The times are simulated.
512 devices in a mesh: pp: 16 (over z), ep: 32 (over y, x, core).
Axes of the slice: x: 4, y: 4, z: 16, core: 2. Of those that a mesh axis runs over, the one named last changes fastest.
Arguments:
- fwd_act: bfloat16 [32768, 3584], P(('pp', 'ep')), may hold values from -6 to 6
- fwd_ids: int32 [32768, 1], P(('pp', 'ep')), may hold values from 0 to 3; in each aligned block of 64 rows (0 to 63, 64 to 127, ...) at most 17 rows name the same one
- bwd_act: bfloat16 [32768, 3584], P(('pp', 'ep')), may hold values from -6 to 6
- bwd_ids: int32 [32768, 1], P(('pp', 'ep')), may hold values from 0 to 3; in each aligned block of 64 rows (0 to 63, 64 to 127, ...) at most 17 rows name the same one
- bwd_grad: bfloat16 [32768, 3584], P(('pp', 'ep')), may hold values from -6 to 6
- norm_gain: bfloat16 [16, 3584], P('pp'), may hold values from 0.099609375 to 1.8984375
- router: bfloat16 [16, 3584, 4], P('pp'), may hold values from -0.09375 to 0.09375
- w_gate: bfloat16 [512, 3584, 128], P(('pp', 'ep')), may hold values from -0.09375 to 0.09375
- w_down: bfloat16 [512, 128, 3584], P(('pp', 'ep')), may hold values from -0.1875 to 0.1875
- saved_gate: bfloat16 [16, 32, 544, 128], P('pp', 'ep'), may hold values from -6 to 6
Outputs:
- fwd_next: bfloat16 [32768, 3584], P(('pp', 'ep'))
- bwd_next: bfloat16 [32768, 3584], P(('pp', 'ep'))
Inputs may be any that keep to these rules, and one draw needn't show every extreme that they name: `fwd_ids`: each row names one held expert. Among the rows of one device no expert is named by more than 17 rows; some device names some expert exactly 17 times. `bwd_ids`: as for fwd_ids.
All inputs are finite; a program needn't handle non-finite values.
Results may differ from a plain program's by a relative error of at most 0.015.
Values may be sent and summed in bfloat16 or wider, within the bound.
A program may use at most 128 MiB of HBM per device.

v0:
```python
import jax
import jax.numpy as jnp
from jax import lax
from jax.sharding import PartitionSpec as P

epsilon = 1e-06
route_scale = 2.5


def shifted(shard, axis, by):
    peers = lax.axis_size(axis)
    return lax.ppermute(shard, axis, [(i, (i + by) % peers) for i in range(peers)])


def normalize(act, gain_row):
    values = act.astype(jnp.float32)
    scaled = lax.rsqrt(jnp.mean(values * values, axis=-1, keepdims=True) + epsilon)
    return ((values * scaled * gain_row.astype(jnp.float32)).astype(jnp.bfloat16), scaled)


def gating(normed, router_table, ids):
    logits = jnp.dot(normed, router_table, preferred_element_type=jnp.float32)
    affinity = jax.nn.sigmoid(logits)
    selected = (
        ids[:, :, None] == jnp.arange(router_table.shape[1], dtype=jnp.int32)[None, None, :]
    ).astype(jnp.float32)
    gates = jnp.sum(selected * affinity[:, None, :], axis=-1)
    return (gates, affinity, selected)


def positions(flat_ids, experts):
    onehot = (flat_ids[..., None] == jnp.arange(experts, dtype=jnp.int32)).astype(jnp.int32)
    earlier = jnp.cumsum(onehot, axis=-2) - onehot
    return jnp.sum(earlier * onehot, axis=-1)


def build_send(rows, slot_index, route_count, experts, capacity, split_count):
    repeated = jnp.repeat(rows, route_count, axis=0)
    placed = jnp.zeros((experts * capacity, rows.shape[1]), rows.dtype).at[slot_index].set(repeated)
    return jnp.repeat(placed.reshape(experts, capacity, rows.shape[1]), split_count, axis=0)


def fold_slices(returned, experts, split_count):
    wide = returned.astype(jnp.float32).reshape((experts, split_count) + returned.shape[1:])
    return jnp.sum(wide, axis=1).reshape((-1,) + returned.shape[2:])


def slice_forward(slot_rows, gate_part, down_part):
    gate_proj = jnp.einsum("scd,dh->sch", slot_rows, gate_part, preferred_element_type=jnp.float32)
    hidden = jax.nn.silu(gate_proj).astype(jnp.bfloat16)
    return jnp.einsum("sch,hd->scd", hidden, down_part, preferred_element_type=jnp.float32).astype(
        jnp.bfloat16
    )


def slice_backward(slot_grads, saved_rows, gate_part, down_part):
    gate_proj = saved_rows.astype(jnp.float32)
    hidden = jax.nn.silu(gate_proj).astype(jnp.bfloat16)
    output = jnp.einsum(
        "sch,hd->scd", hidden, down_part, preferred_element_type=jnp.float32
    ).astype(jnp.bfloat16)
    dot_part = jnp.sum(slot_grads.astype(jnp.float32) * output.astype(jnp.float32), axis=-1).astype(
        jnp.bfloat16
    )
    grad_hidden = jnp.einsum(
        "scd,hd->sch", slot_grads, down_part, preferred_element_type=jnp.float32
    )
    sigmoid_gate = jax.nn.sigmoid(gate_proj)
    grad_gate = (grad_hidden * sigmoid_gate * (1.0 + gate_proj * (1.0 - sigmoid_gate))).astype(
        jnp.bfloat16
    )
    grad_part = jnp.einsum(
        "sch,dh->scd", grad_gate, gate_part, preferred_element_type=jnp.float32
    ).astype(jnp.bfloat16)
    return (grad_part, dot_part)


def finish_forward(act, gates, gathered):
    mixed = jnp.sum(gates[:, :, None] * gathered, axis=1)
    return (act.astype(jnp.float32) + route_scale * mixed).astype(jnp.bfloat16)


def finish_backward(
    act, grad, scaled, gain_row, router_table, gates, affinity, selected, grad_rows, dot_terms
):
    route_coef = route_scale * gates
    grad_normed = jnp.sum(route_coef[:, :, None] * grad_rows, axis=1)
    grad_gates = route_scale * dot_terms
    grad_affinity = jnp.sum(selected * grad_gates[:, :, None], axis=1)
    grad_logits = (grad_affinity * affinity * (1.0 - affinity)).astype(jnp.bfloat16)
    grad_normed = grad_normed + jnp.dot(
        grad_logits, router_table.T, preferred_element_type=jnp.float32
    )
    values = act.astype(jnp.float32)
    grad_pre = grad_normed * gain_row.astype(jnp.float32)
    grad_act = scaled * (
        grad_pre - values * scaled * scaled * jnp.mean(grad_pre * values, axis=-1, keepdims=True)
    )
    return (grad.astype(jnp.float32) + grad_act).astype(jnp.bfloat16)


def on_device(
    fwd_act, fwd_ids, bwd_act, bwd_ids, bwd_grad, norm_gain, router, w_gate, w_down, saved_gate
):
    groups = lax.axis_size("ep")
    gain_row = norm_gain[0]
    router_table = router[0]
    experts = router_table.shape[1]
    split_count = groups // experts
    tok_rows, route_count = fwd_ids.shape
    model_width = fwd_act.shape[1]
    capacity = tok_rows // experts + 1
    gate_part = w_gate[0]
    down_part = w_down[0]
    saved_rows = saved_gate.reshape(groups, capacity, saved_gate.shape[-1])
    fwd_normed, fwd_scaled = normalize(fwd_act, gain_row)
    fwd_gates, fwd_aff, fwd_sel = gating(fwd_normed, router_table, fwd_ids)
    fwd_flat = fwd_ids.reshape(-1)
    fwd_place = positions(fwd_flat, experts)
    fwd_slot = fwd_flat * capacity + fwd_place
    bwd_normed, bwd_scaled = normalize(bwd_act, gain_row)
    bwd_gates, bwd_aff, bwd_sel = gating(bwd_normed, router_table, bwd_ids)
    bwd_flat = bwd_ids.reshape(-1)
    bwd_place = positions(bwd_flat, experts)
    bwd_slot = bwd_flat * capacity + bwd_place
    fwd_send = build_send(fwd_normed, fwd_slot, route_count, experts, capacity, split_count)
    grad_send = build_send(bwd_grad, bwd_slot, route_count, experts, capacity, split_count)
    fwd_back = lax.all_to_all(
        slice_forward(
            lax.all_to_all(fwd_send, "ep", split_axis=0, concat_axis=0, tiled=True),
            gate_part,
            down_part,
        ),
        "ep",
        split_axis=0,
        concat_axis=0,
        tiled=True,
    )
    got_grads = lax.all_to_all(grad_send, "ep", split_axis=0, concat_axis=0, tiled=True)
    grad_part, dot_part = slice_backward(got_grads, saved_rows, gate_part, down_part)
    bwd_back, dots_back = (
        lax.all_to_all(grad_part, "ep", split_axis=0, concat_axis=0, tiled=True),
        lax.all_to_all(dot_part, "ep", split_axis=0, concat_axis=0, tiled=True),
    )
    fwd_gathered = fold_slices(fwd_back, experts, split_count)[fwd_slot].reshape(
        tok_rows, route_count, model_width
    )
    fwd_result = finish_forward(fwd_act, fwd_gates, fwd_gathered)
    bwd_rows = fold_slices(bwd_back, experts, split_count)[bwd_slot].reshape(
        tok_rows, route_count, model_width
    )
    bwd_dots = fold_slices(dots_back, experts, split_count)[bwd_slot].reshape(tok_rows, route_count)
    bwd_result = finish_backward(
        bwd_act,
        bwd_grad,
        bwd_scaled,
        gain_row,
        router_table,
        bwd_gates,
        bwd_aff,
        bwd_sel,
        bwd_rows,
        bwd_dots,
    )
    fwd_next = shifted(fwd_result, "pp", 1)
    bwd_next = shifted(bwd_result, "pp", -1)
    return (fwd_next, bwd_next)


def solution(mesh):
    return jax.shard_map(
        on_device,
        mesh=mesh,
        in_specs=(
            P(("pp", "ep"), None),
            P(("pp", "ep"), None),
            P(("pp", "ep"), None),
            P(("pp", "ep"), None),
            P(("pp", "ep"), None),
            P("pp", None),
            P("pp", None, None),
            P(("pp", "ep"), None, None),
            P(("pp", "ep"), None, None),
            P("pp", "ep", None, None),
        ),
        out_specs=(P(("pp", "ep"), None), P(("pp", "ep"), None)),
        check_vma=False,
    )
```

profile of v0, /device:TPU:1, one launch (start us, length us, event | category | flops | bytes accessed | tf_op | source)
XLA Modules:
  0.0 341.3 jit_solution(1893398887485143911)
XLA Ops:
  3.0 1.8 scatter_custom_fusion.1
  5.0 2.8 broadcast_in_dim.5
  7.8 11.5 %all-to-all-start.2 = ((bf16[32,17,3584]{2,1,0:T(8,128)(2,1)}), bf16[32,17,3584]{2,1,0:T(8,128)(2,1)}, u32[]{:S(2)}, u32[]{:S(2)}) async-start(bf16[32,17,3584]{2,1,0:T(8,128)(2,1)} %bitcast.59), calls=%async_computation.2 | async-start | bytes 11010048 | tf_op jit(solution)/shard_map/all_to_all | solution.py:139
  21.6 62.2 %all-to-all-done.2 = bf16[32,17,3584]{2,1,0:T(8,128)(2,1)} async-done(((bf16[32,17,3584]{2,1,0:T(8,128)(2,1)}), bf16[32,17,3584]{2,1,0:T(8,128)(2,1)}, u32[]{:S(2)}, u32[]{:S(2)}) %all-to-all-start.2) | async-done | bytes 3899424 | tf_op jit(solution)/shard_map/all_to_all | solution.py:139
  83.7 2.8 broadcast_in_dim.4
  86.5 9.3 %all-to-all-start = ((bf16[32,17,3584]{2,1,0:T(8,128)(2,1)}), bf16[32,17,3584]{2,1,0:T(8,128)(2,1)}, u32[]{:S(2)}, u32[]{:S(2)}) async-start(bf16[32,17,3584]{2,1,0:T(8,128)(2,1)} %bitcast.60), calls=%async_computation | async-start | bytes 11010048 | tf_op jit(solution)/shard_map/all_to_all | solution.py:130
  96.1 4.3 %multiply_reduce_fusion = bf16[32,17]{0,1:T(8,128)(2,1)S(1)} fusion(bf16[32,17,3584]{2,1,0:T(8,128)(2,1)} %all-to-all-done.2, bf16[1,128,3584]{2,1,0:T(8,128)(2,1)S(1)} %copy-done, bf16[32,17,128]{2,1,0:T(8,128)(2,1)S(1)} %convert_element_type.117), kind=kOutput, calls=%fused_computation.7 | convolution fusion | flops 508870112 | bytes 4957248 | tf_op jit(solution)/shard_map/sch,hd->scd/dot_general | solution.py:59
  101.1 4.1 %fusion.24 = f32[32,17,128]{2,1,0:T(8,128)S(1)} fusion(bf16[32,17,3584]{2,1,0:T(8,128)(2,1)} %all-to-all-done.2, bf16[1,128,3584]{2,1,0:T(8,128)(2,1)S(1)} %copy-done), kind=kOutput, calls=%fused_computation.44 | convolution fusion | flops 499122176 | bytes 5095424 | tf_op jit(solution)/shard_map/scd,hd->sch/dot_general | solution.py:65
  105.3 54.9 %all-to-all-done = bf16[32,17,3584]{2,1,0:T(8,128)(2,1)} async-done(((bf16[32,17,3584]{2,1,0:T(8,128)(2,1)}), bf16[32,17,3584]{2,1,0:T(8,128)(2,1)}, u32[]{:S(2)}, u32[]{:S(2)}) %all-to-all-start) | async-done | bytes 3899424 | tf_op jit(solution)/shard_map/all_to_all | solution.py:130
  160.2 8.2 %all-to-all-start.4 = ((bf16[32,1,17]{2,1,0:T(2,128)(2,1)}), bf16[32,1,17]{2,1,0:T(2,128)(2,1)S(1)}, u32[]{:S(2)}, u32[]{:S(2)}) async-start(bf16[32,1,17]{2,1,0:T(2,128)(2,1)} %copy.42), calls=%async_computation.4 | async-start | bytes 32768 | tf_op jit(solution)/shard_map/all_to_all | solution.py:143
  169.6 4.5 %copy.37 = bf16[32,17,3584]{2,1,0:T(8,128)(2,1)} copy(bf16[32,17,3584]{2,0,1:T(8,128)(2,1)S(1)} %convolution_convert_fusion.1) | data formatting | bytes 7798784 | tf_op jit(solution)/shard_map/convert_element_type | solution.py:74
  175.4 6.3 %all-to-all-start.3 = ((bf16[32,17,3584]{2,1,0:T(8,128)(2,1)}), bf16[32,17,3584]{2,1,0:T(8,128)(2,1)}, u32[]{:S(2)}, u32[]{:S(2)}) async-start(bf16[32,17,3584]{2,1,0:T(8,128)(2,1)} %copy.37), calls=%async_computation.3 | async-start | bytes 11010048 | tf_op jit(solution)/shard_map/all_to_all | solution.py:142
  181.7 4.2 %fusion.28 = f32[32,17,128]{2,1,0:T(8,128)S(1)} fusion(bf16[32,17,3584]{2,1,0:T(8,128)(2,1)} %all-to-all-done, bf16[1,3584,128]{2,1,0:T(8,128)(2,1)S(1)} %copy-done.5), kind=kOutput, calls=%fused_computation.48 | convolution fusion | flops 499122176 | bytes 5095424 | tf_op jit(solution)/shard_map/scd,dh->sch/dot_general | solution.py:49
  187.1 4.6 %copy.29 = bf16[32,17,3584]{2,1,0:T(8,128)(2,1)} copy(bf16[32,17,3584]{2,0,1:T(8,128)(2,1)S(1)} %convolution_convert_fusion.2) | data formatting | bytes 7798784 | tf_op jit(solution)/shard_map/convert_element_type | solution.py:51
  191.7 54.4 %all-to-all-done.3 = bf16[32,17,3584]{2,1,0:T(8,128)(2,1)} async-done(((bf16[32,17,3584]{2,1,0:T(8,128)(2,1)}), bf16[32,17,3584]{2,1,0:T(8,128)(2,1)}, u32[]{:S(2)}, u32[]{:S(2)}) %all-to-all-start.3) | async-done | bytes 3899424 | tf_op jit(solution)/shard_map/all_to_all | solution.py:142
  246.1 9.2 %all-to-all-start.1 = ((bf16[32,17,3584]{2,1,0:T(8,128)(2,1)}), bf16[32,17,3584]{2,1,0:T(8,128)(2,1)}, u32[]{:S(2)}, u32[]{:S(2)}) async-start(bf16[32,17,3584]{2,1,0:T(8,128)(2,1)} %copy.29), calls=%async_computation.1 | async-start | bytes 11010048 | tf_op jit(solution)/shard_map/all_to_all | solution.py:128
  257.1 3.6 %convert_reduce_fusion = f32[4,17,3584]{2,1,0:T(8,128)S(1)} fusion(bf16[32,17,3584]{2,1,0:T(8,128)(2,1)} %all-to-all-done.3), kind=kLoop, calls=%fused_computation.5 | loop fusion | flops 3655680 | bytes 4874240 | tf_op jit(solution)/shard_map/reduce_sum | solution.py:45
  262.3 2.1 fusion.16
  264.4 8.3 %collective-permute-start.1 = (bf16[64,3584]{1,0:T(8,128)(2,1)}, bf16[64,3584]{1,0:T(8,128)(2,1)}, u32[]{:S(2)}, u32[]{:S(2)}) collective-permute-start(bf16[64,3584]{1,0:T(8,128)(2,1)} %fusion.16), channel_id=1, source_target_pairs={{0,480},{32,0},{64,32},{96,64},{128,96},{160,128},{192,160},{224,1... | collective-permute-start | bytes 1376264 | tf_op jit(solution)/shard_map/ppermute | solution.py:12
  272.7 46.9 %all-to-all-done.1 = bf16[32,17,3584]{2,1,0:T(8,128)(2,1)} async-done(((bf16[32,17,3584]{2,1,0:T(8,128)(2,1)}), bf16[32,17,3584]{2,1,0:T(8,128)(2,1)}, u32[]{:S(2)}, u32[]{:S(2)}) %all-to-all-start.1) | async-done | bytes 3899424 | tf_op jit(solution)/shard_map/all_to_all | solution.py:128
  319.6 3.6 %convert_reduce_fusion.1 = f32[4,17,3584]{2,1,0:T(8,128)S(1)} fusion(bf16[32,17,3584]{2,1,0:T(8,128)(2,1)} %all-to-all-done.1), kind=kLoop, calls=%fused_computation.6 | loop fusion | flops 3655680 | bytes 4874240 | tf_op jit(solution)/shard_map/reduce_sum | solution.py:45
  324.6 1.9 collective-permute-start
  326.5 12.2 %collective-permute-done = bf16[64,3584]{1,0:T(8,128)(2,1)S(1)} collective-permute-done((bf16[64,3584]{1,0:T(8,128)(2,1)S(1)}, bf16[64,3584]{1,0:T(8,128)(2,1)S(1)}, u32[]{:S(2)}, u32[]{:S(2)}) %collective-permute-start) | collective-permute-done | bytes 458784 | tf_op jit(solution)/shard_map/ppermute | solution.py:12
  339.5 1.8 copy.65
  (67 shorter events, 14.8 us)
Async XLA Ops:
  0.6 95.4 %copy-start = (bf16[1,128,3584]{2,1,0:T(8,128)(2,1)S(1)}, bf16[1,128,3584]{2,1,0:T(8,128)(2,1)}, u32[]{:S(2)}) copy-start(bf16[1,128,3584]{2,1,0:T(8,128)(2,1)} %param.18) | copy-start | bytes 2752516
  7.8 11.5 %copy-start.10 = (s32[64,1]{0,1:T(1,128)S(1)}, s32[64,1]{0,1:T(1,128)}, u32[]{:S(2)}) copy-start(s32[64,1]{0,1:T(1,128)} %param.11) | copy-start | bytes 772
  7.8 11.8 %copy-start.8 = (bf16[1,3584]{1,0:T(2,128)(2,1)S(1)}, bf16[1,3584]{1,0:T(2,128)(2,1)}, u32[]{:S(2)}) copy-start(bf16[1,3584]{1,0:T(2,128)(2,1)} %param.15) | copy-start | bytes 21508
  7.8 11.9 %copy-start.1 = (bf16[64,3584]{1,0:T(8,128)(2,1)S(1)}, bf16[64,3584]{1,0:T(8,128)(2,1)}, u32[]{:S(2)}) copy-start(bf16[64,3584]{1,0:T(8,128)(2,1)} %param.10) | copy-start | bytes 1376260
  7.8 75.9 %all-to-all-start.2 = ((bf16[32,17,3584]{2,1,0:T(8,128)(2,1)}), bf16[32,17,3584]{2,1,0:T(8,128)(2,1)}, u32[]{:S(2)}, u32[]{:S(2)}) async-start(bf16[32,17,3584]{2,1,0:T(8,128)(2,1)} %bitcast.59), calls=%async_computation.2 | async-start | bytes 11010048 | tf_op jit(solution)/shard_map/all_to_all | solution.py:139
  86.5 9.3 %copy-start.6 = (bf16[1,1,544,128]{3,2,1,0:T(8,128)(2,1)S(1)}, bf16[1,1,544,128]{3,2,1,0:T(8,128)(2,1)}, u32[]{:S(2)}) copy-start(bf16[1,1,544,128]{3,2,1,0:T(8,128)(2,1)} %param.19) | copy-start | bytes 417796
  86.5 73.7 %all-to-all-start = ((bf16[32,17,3584]{2,1,0:T(8,128)(2,1)}), bf16[32,17,3584]{2,1,0:T(8,128)(2,1)}, u32[]{:S(2)}, u32[]{:S(2)}) async-start(bf16[32,17,3584]{2,1,0:T(8,128)(2,1)} %bitcast.60), calls=%async_computation | async-start | bytes 11010048 | tf_op jit(solution)/shard_map/all_to_all | solution.py:130
  96.1 72.4 %copy-start.5 = (bf16[1,3584,128]{2,1,0:T(8,128)(2,1)S(1)}, bf16[1,3584,128]{2,1,0:T(8,128)(2,1)}, u32[]{:S(2)}) copy-start(bf16[1,3584,128]{2,1,0:T(8,128)(2,1)} %param.17) | copy-start | bytes 2752516
  160.2 15.2 %all-to-all-start.4 = ((bf16[32,1,17]{2,1,0:T(2,128)(2,1)}), bf16[32,1,17]{2,1,0:T(2,128)(2,1)S(1)}, u32[]{:S(2)}, u32[]{:S(2)}) async-start(bf16[32,1,17]{2,1,0:T(2,128)(2,1)} %copy.42), calls=%async_computation.4 | async-start | bytes 32768 | tf_op jit(solution)/shard_map/all_to_all | solution.py:143
  175.4 70.7 %all-to-all-start.3 = ((bf16[32,17,3584]{2,1,0:T(8,128)(2,1)}), bf16[32,17,3584]{2,1,0:T(8,128)(2,1)}, u32[]{:S(2)}, u32[]{:S(2)}) async-start(bf16[32,17,3584]{2,1,0:T(8,128)(2,1)} %copy.37), calls=%async_computation.3 | async-start | bytes 11010048 | tf_op jit(solution)/shard_map/all_to_all | solution.py:142
  191.7 63.6 %copy-start.3 = (bf16[64,3584]{1,0:T(8,128)(2,1)S(1)}, bf16[64,3584]{1,0:T(8,128)(2,1)}, u32[]{:S(2)}) copy-start(bf16[64,3584]{1,0:T(8,128)(2,1)} %param.12) | copy-start | bytes 1376260
  191.7 63.8 %copy-start.7 = (bf16[1,3584,4]{1,2,0:T(4,128)(2,1)S(1)}, bf16[1,3584,4]{1,2,0:T(4,128)(2,1)}, u32[]{:S(2)}) copy-start(bf16[1,3584,4]{1,2,0:T(4,128)(2,1)} %param.16) | copy-start | bytes 86020
  191.7 64.1 %copy-start.9 = (s32[64,1]{0,1:T(1,128)S(1)}, s32[64,1]{0,1:T(1,128)}, u32[]{:S(2)}) copy-start(s32[64,1]{0,1:T(1,128)} %param.13) | copy-start | bytes 772
  246.1 73.6 %all-to-all-start.1 = ((bf16[32,17,3584]{2,1,0:T(8,128)(2,1)}), bf16[32,17,3584]{2,1,0:T(8,128)(2,1)}, u32[]{:S(2)}, u32[]{:S(2)}) async-start(bf16[32,17,3584]{2,1,0:T(8,128)(2,1)} %copy.29), calls=%async_computation.1 | async-start | bytes 11010048 | tf_op jit(solution)/shard_map/all_to_all | solution.py:128
  260.8 1.0 copy-start.4
  264.4 62.1 %collective-permute-start.1 = (bf16[64,3584]{1,0:T(8,128)(2,1)}, bf16[64,3584]{1,0:T(8,128)(2,1)}, u32[]{:S(2)}, u32[]{:S(2)}) collective-permute-start(bf16[64,3584]{1,0:T(8,128)(2,1)} %fusion.16), channel_id=1, source_target_pairs={{0,480},{32,0},{64,32},{96,64},{128,96},{160,128},{192,160},{224,1... | collective-permute-start | bytes 1376264 | tf_op jit(solution)/shard_map/ppermute | solution.py:12
  323.4 1.0 copy-start.2
  324.6 14.1 %collective-permute-start = (bf16[64,3584]{1,0:T(8,128)(2,1)S(1)}, bf16[64,3584]{1,0:T(8,128)(2,1)S(1)}, u32[]{:S(2)}, u32[]{:S(2)}) collective-permute-start(bf16[64,3584]{1,0:T(8,128)(2,1)S(1)} %fusion.20), channel_id=1, source_target_pairs={{0,32},{32,64},{64,96},{96,128},{128,160},{160,192},{192,224},{224... | collective-permute-start | bytes 1376264 | tf_op jit(solution)/shard_map/ppermute | solution.py:12
where the time goes:
time: 348 us; the launch traced here: 341 us
  waiting for transfers between devices  232 us (67%)
  starting transfers between devices  54.7 us (16%)
  local copies, waits for them, and re-layouts  23.8 us (7%)
  matrix products  16.1 us (5%)
  other arithmetic  13.8 us (4%)
    all_to_all x1, waiting for transfers between devices, on_device(): lax.all_to_all(grad_send, 'ep', split_axis=0, concat_axis=0, tiled=True)  62.2 us
    all_to_all x1, waiting for transfers between devices, on_device(): lax.all_to_all(fwd_send, 'ep', split_axis=0, concat_axis=0, tiled=True)  54.9 us
    all_to_all x1, waiting for transfers between devices, on_device(): lax.all_to_all(grad_part, 'ep', split_axis=0, concat_axis=0, tiled=True)  54.4 us
    all_to_all x1, waiting for transfers between devices, on_device(): lax.all_to_all(slice_forward(lax.all_to_all(fwd_send, 'ep', split_axis=0,...  46.9 us
    ppermute x2, waiting for transfers between devices, shifted(): lax.ppermute(shard, axis, [(i, (i + by) % peers) for i in range(peers)])  12.2 us
    all_to_all x1, starting transfers between devices, on_device(): lax.all_to_all(grad_send, 'ep', split_axis=0, concat_axis=0, tiled=True)  11.5 us
    ppermute x2, starting transfers between devices, shifted(): lax.ppermute(shard, axis, [(i, (i + by) % peers) for i in range(peers)])  10.2 us
    all_to_all x1, starting transfers between devices, on_device(): lax.all_to_all(fwd_send, 'ep', split_axis=0, concat_axis=0, tiled=True)  9.33 us
  transfers between devices with their start and end apart: 7, of which 6 were waited for; matrix products, arithmetic and copies ran while one was open for 12% of the time, Pallas kernels for 0%

commit v1 on v0

v1 whole, which is shorter than its diff:
```python
import functools

import jax
import jax.numpy as jnp
from jax import lax
from jax.experimental import pallas as pl
from jax.experimental.pallas import tpu as pltpu
from jax.sharding import PartitionSpec as P

MESH = pl.DeviceIdType.MESH
bf16 = jnp.bfloat16
f32 = jnp.float32
epsilon = 1e-06
route_scale = 2.5

TOK = 64
CAP = 17
EXP = 4
PACK = 48
BLK = 144
DOTROW = 34
HS = 128
NCH = 2
MIRROR = (0, 2, 1, 3)


def iota(shape, dim):
    return lax.broadcasted_iota(jnp.int32, shape, dim)


def mm(a, b):
    return lax.dot_general(a, b, (((1,), (0,)), ((), ())), preferred_element_type=f32)


def mm_nt(a, b):
    return lax.dot_general(a, b, (((1,), (1,)), ((), ())), preferred_element_type=f32)


def group_of(q):
    return (q >= 17).astype(jnp.int32) + (q >= 34).astype(jnp.int32) + (q >= 51).astype(jnp.int32)


def kernel(
    fa, fid, ba, bid, bg, gain, rt, wg_hbm, wd_hbm, saved,
    fout, bout,
    S, RY, A, WG, WD, zo, zs, zr, hs, hr, o3, relay, o1, o2, fup, fdn, TS, TR,
    fst, bst, gpre, svp, oh, dots,
    wl, wsend, wrecv, dloc, dsend, drecv, asend, arecv, zsend, zrecv, hsend, hrecv,
    rsend, rrecv, tloc, tsend, trecv, osend, orecv,
):
    D = fa.shape[1]
    HF = D // 2
    CW = HF // NCH
    n_pp = lax.axis_size("pp")
    pp = lax.axis_index("pp")
    ep = lax.axis_index("ep")
    y = ep // 8
    x = (ep // 2) % 4
    c = ep % 2

    def dev(yy, xx, cc):
        return (pp, (yy * 4 + xx) * 2 + cc)

    up = 1 + 2 * c
    x_up = (x + up) % 4
    x_dn = (x + 4 - up) % 4
    x_op = (x + 2) % 4
    d_up = dev(y, x_up, c)
    d_dn = dev(y, x_dn, c)
    d_sib = dev(y, x, 1 - c)
    d_zn = ((pp + 1) % n_pp, ep)
    d_zp = ((pp + n_pp - 1) % n_pp, ep)
    others = [(dy, dc) for dy in range(4) for dc in range(2) if (dy, dc) != (0, 0)]

    def remote(src, dst, ssem, rsem, device):
        return pltpu.make_async_remote_copy(
            src_ref=src, dst_ref=dst, send_sem=ssem, recv_sem=rsem, device_id=device, device_id_type=MESH
        )

    barrier = pltpu.get_barrier_semaphore()
    partners = [dev((y + dy) % 4, x, (c + dc) % 2) for dy, dc in others] + [d_up, d_dn, d_zn, d_zp]
    for partner in partners:
        pl.semaphore_signal(barrier, inc=1, device_id=partner, device_id_type=MESH)

    mine = pl.multiple_of(c * HF, 128)
    yours = pl.multiple_of((1 - c) * HF, 128)
    own_w = [
        pltpu.make_async_copy(wg_hbm.at[pl.ds(mine, HF), :], WG.at[:, pl.ds(0, HS)], wl.at[0]),
        pltpu.make_async_copy(wd_hbm.at[:, pl.ds(mine, HF)], WD.at[pl.ds(0, HS), :], wl.at[1]),
    ]
    for copy in own_w:
        copy.start()

    def cols(k):
        return slice(k * CW, (k + 1) * CW)

    def inverse(h_ref):
        total = jnp.zeros((TOK, 1), f32)
        for k in range(2 * NCH):
            v = h_ref[:, cols(k)].astype(f32)
            total = total + jnp.sum(v * v, axis=-1, keepdims=True)
        return lax.rsqrt(total * (1.0 / D) + epsilon)

    def normed(h_ref, inv, k):
        return (h_ref[:, cols(k)].astype(f32) * inv * gain[:, cols(k)].astype(f32)).astype(bf16)

    below = (iota((TOK, TOK), 0) > iota((TOK, TOK), 1)).astype(f32).astype(bf16)

    def routes(id_ref, base):
        ids = id_ref[...]
        onehot = (ids == iota((TOK, 16), 1)).astype(f32)
        earlier = mm(below, onehot.astype(bf16))
        place = jnp.sum(onehot * earlier, axis=-1, keepdims=True)
        column = ids.astype(f32) * PACK + place + base
        spread = (column == iota((TOK, 256), 1).astype(f32)).astype(f32)
        return onehot, place, spread

    f_one, f_place, f_spread = routes(fid, 0.0)
    b_one, b_place, b_spread = routes(bid, 17.0)
    spread = jnp.concatenate([f_spread, b_spread], axis=0)
    oh[...] = spread.astype(bf16)
    packer = spread.T[: EXP * PACK].astype(bf16)
    f_inv = inverse(fa)

    def send_desc(ch, dy, dc):
        e, c2 = (y + dy) % 4, (c + dc) % 2
        return remote(S.at[ch, c2, e], RY.at[ch, c, y], dsend.at[ch, dy, dc], drecv.at[ch, c, y], dev(e, x, c2))

    def arrive(buf, sem):
        remote(buf, buf, sem, sem, d_sib).wait_recv()

    logits = jnp.zeros((TOK, 16), f32)
    for ch in range(NCH):
        for c2 in range(2):
            k = c2 * NCH + ch
            norm = normed(fa, f_inv, k)
            both = jnp.concatenate([norm, bg[:, cols(k)]], axis=0)
            S[ch, c2] = mm(packer, both).astype(bf16).reshape(EXP, PACK, CW)
            logits = logits + mm_nt(norm, rt[:, cols(k)])
        if ch == 0:
            pl.semaphore_wait(barrier, len(partners))
        for dy, dc in others:
            send_desc(ch, dy, dc).start()
        pltpu.make_async_copy(S.at[ch, c, y], RY.at[ch, c, y], dloc.at[ch]).start()
    give_w = [
        remote(wg_hbm.at[pl.ds(yours, HF), :], WG.at[:, pl.ds(HS, HS)], wsend.at[0], wrecv.at[0], d_sib),
        remote(wd_hbm.at[:, pl.ds(yours, HF)], WD.at[pl.ds(HS, HS), :], wsend.at[1], wrecv.at[1], d_sib),
    ]
    for copy in give_w:
        copy.start()
    f_gate = jnp.sum(f_one * jax.nn.sigmoid(logits), axis=-1, keepdims=True)

    r = iota((BLK, 1), 0)
    q = r - 68
    want = jnp.where(r < 68, r + 31 * group_of(r), jnp.where(r < 136, q + 31 * group_of(q) + 17, -1))
    compact = (want == iota((BLK, EXP * PACK), 1)).astype(f32).astype(bf16)

    def ag_own(ch):
        return [
            remote(A.at[0, ch], A.at[1, ch], asend.at[0, ch], arecv.at[0, ch], d_up),
            remote(A.at[0, ch], A.at[2, ch], asend.at[1, ch], arecv.at[1, ch], d_dn),
        ]

    def ag_on(ch):
        return remote(A.at[1, ch], A.at[3, ch], asend.at[2, ch], arecv.at[2, ch], d_up)

    for ch in range(NCH):
        for dy, dc in others:
            sy, sc = (y + dy) % 4, (c + dc) % 2
            arrive(RY.at[ch, sc, sy], drecv.at[ch, sc, sy])
        pltpu.make_async_copy(S.at[ch, c, y], RY.at[ch, c, y], dloc.at[ch]).wait()
        for sc in range(2):
            A[0, ch, sc * BLK : (sc + 1) * BLK] = mm(compact, RY[ch, sc].reshape(EXP * PACK, CW)).astype(bf16)
        for copy in ag_own(ch):
            copy.start()

    b_inv = inverse(ba)
    logits = jnp.zeros((TOK, 16), f32)
    for k in range(2 * NCH):
        logits = logits + mm_nt(normed(ba, b_inv, k), rt[:, cols(k)])
    b_aff = jax.nn.sigmoid(logits)
    b_gate = jnp.sum(b_one * b_aff, axis=-1, keepdims=True)
    svp[0 : saved.shape[0]] = saved[...]
    svp[saved.shape[0] :] = jnp.zeros((svp.shape[0] - saved.shape[0], HS), bf16)
    kind = iota((2 * BLK, 1), 0)
    kind = jnp.where(kind >= BLK, kind - BLK, kind)
    is_f = kind < 68
    saved_at = jnp.where((r >= 68) & (r < 136), q + 119 * group_of(q), -100000)

    for copy in own_w:
        copy.wait()
    arrive(WG.at[:, pl.ds(HS, HS)], wrecv.at[0])
    arrive(WD.at[pl.ds(HS, HS), :], wrecv.at[1])

    def z_copy(s):
        return remote(zs.at[s], zr.at[MIRROR[s]], zsend.at[s], zrecv.at[MIRROR[s]], d_sib)

    def h_copy(s):
        return remote(hs.at[s], hr.at[MIRROR[s]], hsend.at[s], hrecv.at[MIRROR[s]], d_sib)

    def project(s):
        zg = jnp.zeros((2 * BLK, 2 * HS), f32)
        zd = jnp.zeros((2 * BLK, 2 * HS), f32)
        for ch in range(NCH):
            rows = A[s, ch]
            zg = zg + mm(rows, WG[cols(ch), :])
            zd = zd + mm_nt(rows, WD[:, cols(ch)])
        z = jnp.where(is_f, zg, zd)
        zo[s] = z[:, :HS]
        zs[s] = z[:, HS:]
        z_copy(s).start()

    def activate(s, xs):
        arrive(zr.at[s], zrecv.at[s])
        z = zo[s] + zr[s]
        lanes = iota((BLK, svp.shape[0]), 1)
        picks = [
            (lanes - 17 * (xs * 2 + sc) == saved_at).astype(f32).astype(bf16) for sc in range(2)
        ]
        sv = mm(jnp.concatenate(picks, axis=0), svp[...])
        base = jnp.where(is_f, z, sv)
        sig = jax.nn.sigmoid(base)
        hid = (base * sig).astype(bf16)
        gg = (z * sig * (1.0 + sv * (1.0 - sig))).astype(bf16)
        hs[s] = jnp.where(is_f, hid.astype(f32), gg.astype(f32)).astype(bf16)
        h_copy(s).start()
        prod = jnp.where(is_f, 0.0, hid.astype(f32) * z)
        prod = jnp.concatenate([prod, jnp.zeros((96, HS), f32)], axis=0)
        dots[s] = lax.dot_general(
            jnp.ones((8, HS), f32), prod, (((1,), (1,)), ((), ())),
            preferred_element_type=f32, precision=lax.Precision.HIGHEST,
        )

    def produce(s, ch):
        h = jnp.concatenate([hs[s].astype(f32), hr[s].astype(f32)], axis=1)
        hf = jnp.where(is_f, h, 0.0).astype(bf16)
        hb = jnp.where(is_f, 0.0, h).astype(bf16)
        out = mm(hf, WD[:, cols(ch)]) + mm_nt(hb, WG[cols(ch), :])
        if ch == 0:
            spare = jnp.concatenate([dots[s], jnp.zeros((8, CW - 384), f32)], axis=1)
            out = jnp.concatenate([out[:136], spare, out[144:280], spare], axis=0)
        return out

    def down3(ch):
        return remote(o3.at[ch], relay.at[ch], rsend.at[0, ch], rrecv.at[0, ch], d_dn)

    def down1(ch):
        return remote(o1.at[ch], fup.at[ch], rsend.at[1, ch], rrecv.at[1, ch], d_dn)

    def up2(ch):
        return remote(o2.at[ch], fdn.at[ch], rsend.at[2, ch], rrecv.at[2, ch], d_up)

    project(0)
    for ch in range(NCH):
        arrive(A.at[1, ch], arecv.at[0, ch])
        ag_on(ch).start()
    activate(0, x)
    project(1)
    for ch in range(NCH):
        arrive(A.at[2, ch], arecv.at[1, ch])
    project(2)
    activate(1, x_dn)
    activate(2, x_up)
    arrive(hr.at[2], hrecv.at[2])
    for ch in range(NCH):
        o2[ch] = produce(2, ch).astype(bf16)
        up2(ch).start()
    for ch in range(NCH):
        arrive(A.at[3, ch], arecv.at[2, ch])
    project(3)
    activate(3, x_op)
    arrive(hr.at[3], hrecv.at[3])
    for ch in range(NCH):
        o3[ch] = produce(3, ch).astype(bf16)
        down3(ch).start()
    arrive(hr.at[1], hrecv.at[1])
    for ch in range(NCH):
        arrive(relay.at[ch], rrecv.at[0, ch])
        o1[ch] = (produce(1, ch) + relay[ch].astype(f32)).astype(bf16)
        down1(ch).start()
    arrive(hr.at[0], hrecv.at[0])

    k = iota((EXP * PACK, 1), 0)
    ky = (k >= 48).astype(jnp.int32) + (k >= 96).astype(jnp.int32) + (k >= 144).astype(jnp.int32)
    i = k - 48 * ky
    source = jnp.where(
        i < 17, 17 * ky + i, jnp.where(i < 34, 51 + 17 * ky + i, jnp.where(i == DOTROW, 136, -1))
    )
    expand = (source == iota((EXP * PACK, BLK), 1)).astype(f32).astype(bf16)

    def back_desc(ch, dy, dc):
        ty, tc = (y + dy) % 4, (c + dc) % 2
        return remote(TS.at[ch, tc, ty], TR.at[ch, c, y], tsend.at[ch, dy, dc], trecv.at[ch, c, y], dev(ty, x, tc))

    for ch in range(NCH):
        out = produce(0, ch)
        arrive(fdn.at[ch], rrecv.at[2, ch])
        arrive(fup.at[ch], rrecv.at[1, ch])
        out = (out + fdn[ch].astype(f32) + fup[ch].astype(f32)).astype(bf16)
        for sc in range(2):
            TS[ch, sc] = mm(expand, out[sc * BLK : (sc + 1) * BLK]).astype(bf16).reshape(EXP, PACK, CW)
        for dy, dc in others:
            back_desc(ch, dy, dc).start()
        pltpu.make_async_copy(TS.at[ch, c, y], TR.at[ch, c, y], tloc.at[ch]).start()

    def fwd_copy(kk):
        return remote(fst.at[:, cols(kk)], fout.at[:, cols(kk)], osend.at[0, kk], orecv.at[0, kk], d_zn)

    def bwd_copy(kk):
        return remote(bst.at[:, cols(kk)], bout.at[:, cols(kk)], osend.at[1, kk], orecv.at[1, kk], d_zp)

    spots = oh[:, : EXP * PACK]
    mean = jnp.zeros((TOK, 1), f32)
    for ch in range(NCH):
        for dy, dc in others:
            ey, hc = (y + dy) % 4, (c + dc) % 2
            arrive(TR.at[ch, hc, ey], trecv.at[ch, hc, ey])
        pltpu.make_async_copy(TS.at[ch, c, y], TR.at[ch, c, y], tloc.at[ch]).wait()
        if ch == 0:
            where_dot = (144 * c + 68 + 17 * y).astype(f32) + b_place
            hit = where_dot == iota((TOK, 384), 1).astype(f32)
            dot = jnp.zeros((TOK, 1), f32)
            for e in range(EXP):
                both = TR[0, 0, e, 32:48, 0:384].astype(f32) + TR[0, 1, e, 32:48, 0:384].astype(f32)
                found = jnp.sum(jnp.where(hit, both[2:3, :], 0.0), axis=-1, keepdims=True)
                dot = dot + b_one[:, e : e + 1] * found
            grad_aff = b_one * (route_scale * dot)
            grad_logits = (grad_aff * b_aff * (1.0 - b_aff)).astype(bf16)
        for c2 in range(2):
            kk = c2 * NCH + ch
            got = mm(spots, TR[ch, c2].reshape(EXP * PACK, CW))
            fst[:, cols(kk)] = (
                fa[:, cols(kk)].astype(f32) + route_scale * (f_gate * got[:TOK])
            ).astype(bf16)
            fwd_copy(kk).start()
            grad_n = (route_scale * b_gate) * got[TOK:] + mm(grad_logits, rt[:, cols(kk)])
            pre = grad_n * gain[:, cols(kk)].astype(f32)
            gpre[:, cols(kk)] = pre
            mean = mean + jnp.sum(pre * ba[:, cols(kk)].astype(f32), axis=-1, keepdims=True)
    factor = b_inv * b_inv * (mean * (1.0 / D))
    for kk in range(2 * NCH):
        grad = b_inv * (gpre[:, cols(kk)] - ba[:, cols(kk)].astype(f32) * factor)
        bst[:, cols(kk)] = (bg[:, cols(kk)].astype(f32) + grad).astype(bf16)
        bwd_copy(kk).start()

    for copy in give_w:
        copy.wait_send()
    for ch in range(NCH):
        for dy, dc in others:
            send_desc(ch, dy, dc).wait_send()
            back_desc(ch, dy, dc).wait_send()
        for copy in ag_own(ch):
            copy.wait_send()
        ag_on(ch).wait_send()
        down3(ch).wait_send()
        down1(ch).wait_send()
        up2(ch).wait_send()
    for s in range(4):
        z_copy(s).wait_send()
        h_copy(s).wait_send()
    for kk in range(2 * NCH):
        fwd_copy(kk).wait()
        bwd_copy(kk).wait()


def on_device(
    fwd_act, fwd_ids, bwd_act, bwd_ids, bwd_grad, norm_gain, router, w_gate, w_down, saved_gate
):
    D = fwd_act.shape[1]
    HF = D // 2
    CW = HF // NCH
    rt = jnp.pad(router[0].T, ((0, 12), (0, 0)))
    saved = saved_gate[0, 0]
    vmem = pl.BlockSpec(memory_space=pltpu.VMEM)
    hbm = pl.BlockSpec(memory_space=pl.ANY)
    dma = pltpu.SemaphoreType.DMA
    V = pltpu.VMEM
    block = (NCH, 2 * BLK, CW)
    return pl.pallas_call(
        kernel,
        out_shape=[jax.ShapeDtypeStruct((TOK, D), bf16)] * 2,
        in_specs=[vmem] * 7 + [hbm] * 2 + [vmem],
        out_specs=[hbm, hbm],
        scratch_shapes=[
            V((NCH, 2, EXP, PACK, CW), bf16),
            V((NCH, 2, EXP, PACK, CW), bf16),
            V((4,) + block, bf16),
            V((HF, 2 * HS), bf16),
            V((2 * HS, HF), bf16),
            V((4, 2 * BLK, HS), f32),
            V((4, 2 * BLK, HS), f32),
            V((4, 2 * BLK, HS), f32),
            V((4, 2 * BLK, HS), bf16),
            V((4, 2 * BLK, HS), bf16),
            V(block, bf16),
            V(block, bf16),
            V(block, bf16),
            V(block, bf16),
            V(block, bf16),
            V(block, bf16),
            V((NCH, 2, EXP, PACK, CW), bf16),
            V((NCH, 2, EXP, PACK, CW), bf16),
            V((TOK, D), bf16),
            V((TOK, D), bf16),
            V((TOK, D), f32),
            V((640, HS), bf16),
            V((2 * TOK, 256), bf16),
            V((4, 8, 384), f32),
            dma((2,)), dma((2,)), dma((2,)),
            dma((NCH,)), dma((NCH, 4, 2)), dma((NCH, 2, 4)),
            dma((3, NCH)), dma((3, NCH)),
            dma((4,)), dma((4,)), dma((4,)), dma((4,)),
            dma((3, NCH)), dma((3, NCH)),
            dma((NCH,)), dma((NCH, 4, 2)), dma((NCH, 2, 4)),
            dma((2, 2 * NCH)), dma((2, 2 * NCH)),
        ],
        compiler_params=pltpu.CompilerParams(
            collective_id=0, has_side_effects=True, vmem_limit_bytes=56 * 2**20
        ),
    )(fwd_act, fwd_ids, bwd_act, bwd_ids, bwd_grad, norm_gain, rt, w_gate[0], w_down[0], saved)


def solution(mesh):
    return jax.shard_map(
        on_device,
        mesh=mesh,
        in_specs=(
            P(("pp", "ep"), None),
            P(("pp", "ep"), None),
            P(("pp", "ep"), None),
            P(("pp", "ep"), None),
            P(("pp", "ep"), None),
            P("pp", None),
            P("pp", None, None),
            P(("pp", "ep"), None, None),
            P(("pp", "ep"), None, None),
            P("pp", "ep", None, None),
        ),
        out_specs=(P(("pp", "ep"), None), P(("pp", "ep"), None)),
        check_vma=False,
    )
```

time: 348 us -> 122 us (0.35); the launches traced: 341 us -> 122 us
  waiting for transfers between devices: 232 us -> 0 us
  Pallas kernels: 0 us -> 116 us
  starting transfers between devices: 54.7 us -> 0 us
  local copies, waits for them, and re-layouts: 23.8 us -> 5.37 us
  matrix products: 16.1 us -> 0 us
  other arithmetic: 13.8 us -> 0 us
    all_to_all x5 -> x0, waiting for transfers between devices: 220 us -> none  [the longest x1 62.2 us: on_device(): lax.all_to_all(grad_send, 'ep', split_axis=0, concat_axis=0, tiled=True)]
    pallas_call x0 -> x1, Pallas kernels: none -> 116 us  [on_device(): pl.pallas_call(kernel, out_shape=[jax.ShapeDtypeStruct((TOK, D), bf16)] *...]
    all_to_all x5 -> x0, starting transfers between devices: 44.5 us -> none  [the longest x1 11.5 us: on_device(): lax.all_to_all(grad_send, 'ep', split_axis=0, concat_axis=0, tiled=True)]
    dot_general x8 -> x0, matrix products: 16.1 us -> none  [the longest x1 4.33 us: slice_backward(): jnp.einsum('sch,hd->scd', hidden, down_part, preferred_element_type=jnp.f...]
    ppermute x2 -> x0, waiting for transfers between devices: 12.2 us -> none  [shifted(): lax.ppermute(shard, axis, [(i, (i + by) % peers) for i in range(peers)])]
    ppermute x2 -> x0, starting transfers between devices: 10.2 us -> none  [shifted(): lax.ppermute(shard, axis, [(i, (i + by) % peers) for i in range(peers)])]
    convert_element_type x7 -> x0, local copies, waits for them, and re-layouts: 10.2 us -> none  [the longest x1 4.58 us: slice_forward(): jnp.einsum('sch,hd->scd', hidden, down_part, preferred_element_type=jnp.f...]
    reduce_sum x7 -> x0, other arithmetic: 8.24 us -> none  [the longest x3 7.14 us: fold_slices(): return jnp.sum(wide, axis=1).reshape((-1,) + returned.shape[2:])]
  transfers between devices with their start and end apart: 7 -> 0, of which waited for: 6 -> 0; matrix products, arithmetic and copies ran while one was open for 12% -> 0% of each run, Pallas kernels for 0% -> 0%
where the time goes in v1:
time: 122 us
  Pallas kernels  116 us (95%)
  local copies, waits for them, and re-layouts  5.37 us (4%)
    pallas_call x1, Pallas kernels, on_device(): pl.pallas_call(kernel, out_shape=[jax.ShapeDtypeStruct((TOK, D), bf16)] *...  116 us
    unnamed x12, local copies, waits for them, and re-layouts  4.71 us

profile of v1, /device:TPU:1, one launch (start us, length us, event | category | flops | bytes accessed | tf_op | source)
XLA Modules:
  0.0 122.2 jit_solution(16749948361392620323)
XLA Ops:
  0.6 0.0 copy-start.2
  0.6 0.6 copy-done.2
  1.3 0.0 copy-start.3
  1.3 0.0 copy-start.1
  1.3 0.7 copy.12.fid
  2.0 0.0 copy-done.3
  2.0 0.7 copy.13.bid
  2.7 0.0 copy-done.1
  2.7 0.7 pad.4.rt
  3.4 116.2 %shard_map.113 = (bf16[64,3584]{1,0:T(8,128)(2,1)}, bf16[64,3584]{1,0:T(8,128)(2,1)}) custom-call(bf16[64,3584]{1,0:T(8,128)(2,1)} %fa.1, s32[64,1]{1,0:T(8,128)} %copy.12.fid, bf16[64,3584]{1,0:T(8,128)(2,1)} %ba.1, s32[64,1]{1,0:T(8,128)} %copy.13.bid, bf16[64,3584]{1,0:T(8,128)(2,1)} %bg.1, bf16[1,3584]{1,0:T(2,128)(2,1)} %gain.1, ...), custom_call_target="tpu_custom_call" | custom-call | tf_op jit(solution)/shard_map/pallas_call | solution.py:379
  119.6 0.0 copy-start
  119.6 1.9 %copy.16 = bf16[64,3584]{1,0:T(8,128)(2,1)} copy(bf16[64,3584]{1,0:T(8,128)(2,1)} %get-tuple-element.4) | data formatting | bytes 917504
  121.5 0.0 copy-done
  121.5 0.8 copy.17
Async XLA Ops:
  0.6 0.7 copy-start.2
  1.3 0.7 copy-start.3
  1.3 1.4 %copy-start.1 = (bf16[1,3584,4]{1,2,0:T(4,128)(2,1)S(1)}, bf16[1,3584,4]{1,2,0:T(4,128)(2,1)}, u32[]{:S(2)}) copy-start(bf16[1,3584,4]{1,2,0:T(4,128)(2,1)} %param.16) | copy-start | bytes 86020
  119.6 1.9 %copy-start = (bf16[64,3584]{1,0:T(8,128)(2,1)S(1)}, bf16[64,3584]{1,0:T(8,128)(2,1)}, u32[]{:S(2)}) copy-start(bf16[64,3584]{1,0:T(8,128)(2,1)} %get-tuple-element.5) | copy-start | bytes 1376260

commit v2 on v0

v2 whole, which is shorter than its diff:
```python
import functools

import jax
import jax.numpy as jnp
from jax import lax
from jax.experimental import pallas as pl
from jax.experimental.pallas import tpu as pltpu
from jax.sharding import PartitionSpec as P

MESH = pl.DeviceIdType.MESH
bf16 = jnp.bfloat16
f32 = jnp.float32
epsilon = 1e-06
route_scale = 2.5

TOK = 64
CAP = 17
EXP = 4
SUB = 256
PACK = 128
BLK = 144
HS = 128
MIRROR = (0, 2, 1, 3)
BWD, FWD = 0, 1


def plan(half):
    pieces = half // SUB
    if pieces == 7:
        return [(0, 32), (32, 32), (64, 32), (96, 32)], [(0, 1), (1, 3), (3, 5), (5, 7)], [(0, 2), (2, 4), (4, 6), (6, 7)]
    return [(0, 32), (32, 96)], [(0, 1), (1, pieces)], [(0, 2), (2, pieces)]


def iota(shape, dim):
    return lax.broadcasted_iota(jnp.int32, shape, dim)


def mm(a, b):
    return lax.dot_general(a, b, (((1,), (0,)), ((), ())), preferred_element_type=f32)


def mm_nt(a, b):
    return lax.dot_general(a, b, (((1,), (1,)), ((), ())), preferred_element_type=f32)


def select(mask):
    return mask.astype(f32).astype(bf16)


def group_of(q):
    return (q >= 17).astype(jnp.int32) + (q >= 34).astype(jnp.int32) + (q >= 51).astype(jnp.int32)


def kernel(
    fa_hbm, fid, ba_hbm, bid, bg_hbm, gain, rt, wg_hbm, wd_hbm, saved,
    fout, bout,
    fa, ba, bg,
    S, RY, A, WG, WD, zo, zs, zr, hx, o3, relay, o1, o2, fup, fdn, fin, TS, TR,
    fst, bst, gpre, svp, dots,
    ld, wl, wsend, wrecv, dloc, dsend, drecv, asend, arecv, zsend, zrecv, hsend, hrecv,
    rsend, rrecv, tloc, tsend, trecv, osend, orecv,
):
    D = fa.shape[1]
    n_saved = saved.shape[0]
    HF = D // 2
    NS = HF // SUB
    CUTS, OUT, BACK = plan(HF)
    NC = range(len(CUTS))
    n_pp = lax.axis_size("pp")
    pp = lax.axis_index("pp")
    ep = lax.axis_index("ep")
    y = ep // 8
    x = (ep // 2) % 4
    c = ep % 2

    def dev(yy, xx, cc):
        return (pp, (yy * 4 + xx) * 2 + cc)

    up = 1 + 2 * c
    x_up = (x + up) % 4
    x_dn = (x + 4 - up) % 4
    x_op = (x + 2) % 4
    d_up = dev(y, x_up, c)
    d_dn = dev(y, x_dn, c)
    d_sib = dev(y, x, 1 - c)
    d_zn = ((pp + 1) % n_pp, ep)
    d_zp = ((pp + n_pp - 1) % n_pp, ep)
    others = [(dy, dc) for dy in range(4) for dc in range(2) if (dy, dc) != (0, 0)]

    def remote(src, dst, ssem, rsem, device):
        return pltpu.make_async_remote_copy(
            src_ref=src, dst_ref=dst, send_sem=ssem, recv_sem=rsem, device_id=device, device_id_type=MESH
        )

    def arrive(buf, sem):
        remote(buf, buf, sem, sem, d_sib).wait_recv()

    barrier = pltpu.get_barrier_semaphore()
    partners = [dev((y + dy) % 4, x, (c + dc) % 2) for dy, dc in others] + [d_up, d_dn, d_zn, d_zp]
    for partner in partners:
        pl.semaphore_signal(barrier, inc=1, device_id=partner, device_id_type=MESH)

    mine = pl.multiple_of(c * HF, 128)
    yours = pl.multiple_of((1 - c) * HF, 128)
    own_w = [
        pltpu.make_async_copy(wg_hbm.at[pl.ds(mine, HF), :], WG.at[:, pl.ds(0, HS)], wl.at[0]),
        pltpu.make_async_copy(wd_hbm.at[:, pl.ds(mine, HF)], WD.at[pl.ds(0, HS), :], wl.at[1]),
    ]
    load_bg, load_fa, load_ba, load_saved = [
        pltpu.make_async_copy(bg_hbm, bg, ld.at[0]),
        pltpu.make_async_copy(fa_hbm, fa, ld.at[1]),
        pltpu.make_async_copy(ba_hbm, ba, ld.at[2]),
        pltpu.make_async_copy(saved, svp.at[pl.ds(0, n_saved)], ld.at[3]),
    ]
    for copy in [load_bg, load_fa] + own_w + [load_ba, load_saved]:
        copy.start()
    give_w = [
        remote(wg_hbm.at[pl.ds(yours, HF), :], WG.at[:, pl.ds(HS, HS)], wsend.at[0], wrecv.at[0], d_sib),
        remote(wd_hbm.at[:, pl.ds(yours, HF)], WD.at[pl.ds(HS, HS), :], wsend.at[1], wrecv.at[1], d_sib),
    ]

    def rows(ch):
        return pl.ds(*CUTS[ch])

    def part(cut):
        return pl.ds(cut[0] * SUB, (cut[1] - cut[0]) * SUB)

    def cols(c2, j):
        return slice(c2 * HF + j * SUB, c2 * HF + (j + 1) * SUB)

    def wide(c2, cut):
        return slice(c2 * HF + cut[0] * SUB, c2 * HF + cut[1] * SUB)

    every = [(c2, j) for j in range(NS) for c2 in range(2)]

    def row_of(j):
        return 1 + 17 * j

    def pieces_in(ch):
        lo, n = CUTS[ch]
        return [j for j in range(NS) if row_of(j) < lo + n and row_of(j) + 17 > lo]

    def span(j):
        hold = [cut for ch, cut in enumerate(CUTS) if j in pieces_in(ch)]
        return hold[0][0], hold[-1][0] + hold[-1][1]

    def inverse(h_ref):
        total = jnp.zeros((TOK, SUB), f32)
        for at in every:
            v = h_ref[:, cols(*at)].astype(f32)
            total = total + v * v
        return lax.rsqrt(jnp.sum(total, axis=-1, keepdims=True) * (1.0 / D) + epsilon)

    def normed(h_ref, inv, at):
        return (h_ref[:, cols(*at)].astype(f32) * inv * gain[:, cols(*at)].astype(f32)).astype(bf16)

    before = select(iota((TOK, TOK), 0) < iota((TOK, TOK), 1))
    eye = select(iota((TOK, TOK), 0) == iota((TOK, TOK), 1))

    def routes(id_ref):
        ids = id_ref[...]
        onehot = (iota((16, TOK), 0) == ids).astype(f32)
        earlier = mm(onehot.astype(bf16), before)
        place = jnp.sum(onehot * earlier, axis=0, keepdims=True)
        return onehot, place, ids.astype(f32)

    def columns(onehot, place, ids):
        line = iota((16, TOK), 0)
        both = jnp.where(line == 0, ids, jnp.where(line == 1, place, 0.0))
        turned = mm_nt(eye, both.astype(bf16))
        one = mm_nt(eye, onehot.astype(bf16))[:, :EXP]
        return one, turned[:, 1:2], turned[:, 0:1]

    def send_desc(m, ch, dy, dc):
        e, c2 = (y + dy) % 4, (c + dc) % 2
        return remote(
            S.at[m, c2, e, rows(ch)], RY.at[m, c, y, rows(ch)],
            dsend.at[m, ch, dy, dc], drecv.at[m, ch, c, y], dev(e, x, c2),
        )

    def keep_desc(m, ch):
        return pltpu.make_async_copy(S.at[m, c, y, rows(ch)], RY.at[m, c, y, rows(ch)], dloc.at[m, ch])

    def dispatch(m, ch, table, token_rows):
        lo, n = CUTS[ch]
        k = iota((EXP * n, 1), 0)
        k = (k + (PACK - n) * (k // n) + lo).astype(f32)
        picks = [(j, select(k == table[2] * PACK + (table[1] + row_of(j)))) for j in pieces_in(ch)]
        for c2 in range(2):
            filled = jnp.zeros((EXP * n, SUB), f32)
            for j, pick in picks:
                filled = filled + mm(pick, token_rows(c2, j))
            S[m, c2, :, rows(ch)] = filled.astype(bf16).reshape(EXP, n, SUB)
        if (m, ch) == (BWD, 0):
            pl.semaphore_wait(barrier, len(partners))
        for dy, dc in others:
            send_desc(m, ch, dy, dc).start()
        keep_desc(m, ch).start()

    b_routes = routes(bid)
    load_bg.wait()
    for ch in NC:
        dispatch(BWD, ch, b_routes, lambda c2, j: bg[:, cols(c2, j)])
    for copy in give_w:
        copy.start()

    r = iota((BLK, 1), 0)
    core = (r >= 68).astype(jnp.int32)
    q = r - 68 * core
    q_y = group_of(q)

    def compact(j):
        lo, hi = span(j)
        want = jnp.where(r < 136, (core * 4 + q_y) * (hi - lo) + (q - 17 * q_y) + (row_of(j) - lo), -1)
        return select(want == iota((BLK, 8 * (hi - lo)), 1))

    def ag_own(m, ch):
        at = part(OUT[ch])
        src = A.at[m, 0, :, at]
        return [
            remote(src, A.at[m, 1, :, at], asend.at[m, 0, ch], arecv.at[m, 0, ch], d_up),
            remote(src, A.at[m, 2, :, at], asend.at[m, 1, ch], arecv.at[m, 1, ch], d_dn),
        ]

    def ag_on(m, ch):
        at = part(OUT[ch])
        return remote(A.at[m, 1, :, at], A.at[m, 3, :, at], asend.at[m, 2, ch], arecv.at[m, 2, ch], d_up)

    def gather(m, ch):
        for dy, dc in others:
            sy, sc = (y + dy) % 4, (c + dc) % 2
            arrive(RY.at[m, sc, sy, rows(ch)], drecv.at[m, ch, sc, sy])
        keep_desc(m, ch).wait()
        for j in range(*OUT[ch]):
            lo, hi = span(j)
            packs = RY[m, :, :, lo:hi].reshape(8 * (hi - lo), SUB)
            A[m, 0, :, j * SUB : (j + 1) * SUB] = mm(compact(j), packs).astype(bf16)
        for copy in ag_own(m, ch):
            copy.start()

    def pass_on(m, ch):
        arrive(A.at[m, 1, :, part(OUT[ch])], arecv.at[m, 0, ch])
        ag_on(m, ch).start()

    def have(m, slot):
        for ch in NC:
            arrive(A.at[m, slot, :, part(OUT[ch])], arecv.at[m, slot - 1, ch])

    def z_copy(m, s):
        o = MIRROR[s]
        return remote(zs.at[m, s], zr.at[m, o], zsend.at[m, s], zrecv.at[m, o], d_sib)

    def h_copy(m, s):
        o = MIRROR[s]
        return remote(
            hx.at[m, s, :, pl.ds(0, HS)], hx.at[m, o, :, pl.ds(HS, HS)], hsend.at[m, s], hrecv.at[m, o], d_sib
        )

    def project(m, s):
        z = mm(A[m, s], WG[...]) if m == FWD else mm_nt(A[m, s], WD[...])
        zo[m, s] = z[:, :HS]
        zs[m, s] = z[:, HS:]
        z_copy(m, s).start()

    saved_at = jnp.where(r < 136, q + 119 * q_y + 17 * core, -100000)

    def activate(m, s, xs):
        arrive(zr.at[m, s], zrecv.at[m, s])
        z = zo[m, s] + zr[m, s]
        if m == FWD:
            hx[m, s, :, :HS] = (z * jax.nn.sigmoid(z)).astype(bf16)
            h_copy(m, s).start()
            return
        sv = mm(select(iota((BLK, svp.shape[0]), 1) - 34 * xs == saved_at), svp[...])
        sig = jax.nn.sigmoid(sv)
        hx[m, s, :, :HS] = (z * sig * (1.0 + sv * (1.0 - sig))).astype(bf16)
        h_copy(m, s).start()
        prod = (sv * sig).astype(bf16).astype(f32) * z
        prod = jnp.concatenate([prod, jnp.zeros((256 - BLK, HS), f32)], axis=0)
        dots[s] = lax.dot_general(
            jnp.ones((8, HS), f32), prod, (((1,), (1,)), ((), ())),
            preferred_element_type=f32, precision=lax.Precision.HIGHEST,
        )

    def ready(m, s):
        arrive(hx.at[m, s, :, pl.ds(HS, HS)], hrecv.at[m, s])

    def produce(m, s, ch):
        lo, w = BACK[ch][0] * SUB, (BACK[ch][1] - BACK[ch][0]) * SUB
        if m == FWD:
            return mm(hx[m, s], WD[:, lo : lo + w])
        out = mm_nt(hx[m, s], WG[lo : lo + w, :])
        if ch == 0:
            spare = dots[s]
            if w > 256:
                spare = jnp.concatenate([spare, jnp.zeros((8, w - 256), f32)], axis=1)
            out = jnp.concatenate([out[:136], spare], axis=0)
        return out

    def leg(k, src, dst, device):
        def copy(m, ch):
            at = part(BACK[ch])
            return remote(src.at[m, :, at], dst.at[m, :, at], rsend.at[m, k, ch], rrecv.at[m, k, ch], device)

        return copy

    down3 = leg(0, o3, relay, d_dn)
    down1 = leg(1, o1, fup, d_dn)
    up2 = leg(2, o2, fdn, d_up)

    def give2(m, ch):
        o2[m, :, part(BACK[ch])] = produce(m, 2, ch).astype(bf16)
        up2(m, ch).start()

    def give3(m, ch):
        o3[m, :, part(BACK[ch])] = produce(m, 3, ch).astype(bf16)
        down3(m, ch).start()

    def give1(m, ch):
        at = part(BACK[ch])
        own = produce(m, 1, ch)
        arrive(relay.at[m, :, at], rrecv.at[m, 0, ch])
        o1[m, :, at] = (own + relay[m, :, at].astype(f32)).astype(bf16)
        down1(m, ch).start()

    def back_desc(m, ch, dy, dc):
        ty, tc = (y + dy) % 4, (c + dc) % 2
        return remote(
            TS.at[m, tc, ty, rows(ch)], TR.at[m, c, y, rows(ch)],
            tsend.at[m, ch, dy, dc], trecv.at[m, ch, c, y], dev(ty, x, tc),
        )

    def stay_desc(m, ch):
        return pltpu.make_async_copy(TS.at[m, c, y, rows(ch)], TR.at[m, c, y, rows(ch)], tloc.at[m, ch])

    def give0(m, ch):
        at = part(BACK[ch])
        out = produce(m, 0, ch)
        arrive(fdn.at[m, :, at], rrecv.at[m, 2, ch])
        out = out + fdn[m, :, at].astype(f32)
        arrive(fup.at[m, :, at], rrecv.at[m, 1, ch])
        fin[m, :, at] = (out + fup[m, :, at].astype(f32)).astype(bf16)
        lo, n = CUTS[ch]
        k = iota((8 * n, 1), 0)
        owner = k // n
        g = k - n * owner + lo
        filled = jnp.zeros((8 * n, SUB), f32)
        for j in pieces_in(ch):
            first = row_of(j)
            source = jnp.where((g >= first) & (g < first + 17), 17 * owner + g - first, -1)
            if m == BWD and j == 0:
                source = jnp.where(g == 0, 136, source)
            filled = filled + mm(select(source == iota((8 * n, BLK), 1)), fin[m, :, j * SUB : (j + 1) * SUB])
        TS[m, :, :, rows(ch)] = filled.astype(bf16).reshape(2, EXP, n, SUB)
        for dy, dc in others:
            back_desc(m, ch, dy, dc).start()
        stay_desc(m, ch).start()

    def returned(m, ch):
        for dy, dc in others:
            ey, hc = (y + dy) % 4, (c + dc) % 2
            arrive(TR.at[m, hc, ey, rows(ch)], trecv.at[m, ch, hc, ey])
        stay_desc(m, ch).wait()

    def rows_of(m, table, at):
        c2, j = at
        lo, hi = span(j)
        spot = table[2] * (hi - lo) + (table[1] + (row_of(j) - lo))
        spots = select(spot == iota((TOK, EXP * (hi - lo)), 1).astype(f32))
        return mm(spots, TR[m, c2, :, lo:hi].reshape(EXP * (hi - lo), SUB))

    def fwd_copy(c2, ch):
        at = wide(c2, OUT[ch])
        return remote(fst.at[:, at], fout.at[:, at], osend.at[1, c2, ch], orecv.at[1, c2, ch], d_zn)

    def bwd_copy(c2, ch):
        at = wide(c2, OUT[ch])
        return remote(bst.at[:, at], bout.at[:, at], osend.at[0, c2, ch], orecv.at[0, c2, ch], d_zp)

    for ch in NC:
        gather(BWD, ch)
    f_routes = routes(fid)
    load_fa.wait()
    f_inv = inverse(fa)
    for at in every:
        fst[:, cols(*at)] = normed(fa, f_inv, at)
    for ch in NC:
        dispatch(FWD, ch, f_routes, lambda c2, j: fst[:, cols(c2, j)])
    for ch in NC:
        pass_on(BWD, ch)
        gather(FWD, ch)

    f_table = columns(*f_routes)
    b_table = columns(*b_routes)
    b_one, b_place = b_table[:2]
    f_aff = jax.nn.sigmoid(mm_nt(fst[...], rt[...]))
    f_gate = jnp.sum(f_table[0] * f_aff, axis=-1, keepdims=True)
    load_ba.wait()
    load_saved.wait()
    svp[n_saved:] = jnp.zeros((svp.shape[0] - n_saved, HS), bf16)
    for copy in own_w:
        copy.wait()
    arrive(WG.at[:, pl.ds(HS, HS)], wrecv.at[0])
    arrive(WD.at[pl.ds(HS, HS), :], wrecv.at[1])
    project(BWD, 0)
    project(BWD, 1)
    b_inv = inverse(ba)
    for at in every:
        bst[:, cols(*at)] = normed(ba, b_inv, at)
    b_aff = jax.nn.sigmoid(mm_nt(bst[...], rt[...]))
    b_gate = jnp.sum(b_one * b_aff, axis=-1, keepdims=True)
    pass_on(FWD, 0)
    have(BWD, 2)
    project(BWD, 2)
    activate(BWD, 0, x)
    activate(BWD, 1, x_dn)
    activate(BWD, 2, x_up)
    for ch in NC[1:]:
        pass_on(FWD, ch)
    project(FWD, 0)
    project(FWD, 1)
    ready(BWD, 2)
    for ch in NC:
        give2(BWD, ch)
    have(BWD, 3)
    project(BWD, 3)
    activate(FWD, 0, x)
    activate(BWD, 3, x_op)
    ready(BWD, 3)
    for ch in NC:
        give3(BWD, ch)
    have(FWD, 2)
    project(FWD, 2)
    activate(FWD, 1, x_dn)
    activate(FWD, 2, x_up)
    ready(BWD, 1)
    for ch in NC:
        give1(BWD, ch)
    have(FWD, 3)
    project(FWD, 3)
    activate(FWD, 3, x_op)
    ready(FWD, 2)
    ready(FWD, 3)
    n = len(NC)
    for ch in NC[: min(3, n)]:
        give3(FWD, ch)
    for ch in NC[: min(2, n)]:
        give2(FWD, ch)
    ready(BWD, 0)
    for ch in NC:
        give0(BWD, ch)
    ready(FWD, 1)
    ready(FWD, 0)
    mean = jnp.zeros((TOK, SUB), f32)
    grad_logits = None
    for ch in NC:
        give1(FWD, ch)
        if ch + 3 < n:
            give3(FWD, ch + 3)
        if ch + 2 < n:
            give2(FWD, ch + 2)
        returned(BWD, ch)
        if ch == 0:
            hit = (68 * c + 17 * y).astype(f32) + b_place == iota((TOK, SUB), 1).astype(f32)
            dot = jnp.zeros((TOK, 1), f32)
            for e in range(EXP):
                both = TR[BWD, 0, e, 0:16].astype(f32) + TR[BWD, 1, e, 0:16].astype(f32)
                found = jnp.sum(jnp.where(hit, both[0:1, :], 0.0), axis=-1, keepdims=True)
                dot = dot + b_one[:, e : e + 1] * found
            grad_aff = b_one * (route_scale * dot)
            grad_logits = (grad_aff * b_aff * (1.0 - b_aff)).astype(bf16)
        for at in [(c2, j) for j in range(*OUT[ch]) for c2 in range(2)]:
            grad_n = (route_scale * b_gate) * rows_of(BWD, b_table, at) + mm(grad_logits, rt[:, cols(*at)])
            pre = grad_n * gain[:, cols(*at)].astype(f32)
            gpre[:, cols(*at)] = pre
            mean = mean + pre * ba[:, cols(*at)].astype(f32)
        if ch >= 2:
            give0(FWD, ch - 2)
    factor = b_inv * b_inv * (jnp.sum(mean, axis=-1, keepdims=True) * (1.0 / D))
    for ch in NC:
        for c2 in range(2):
            at = wide(c2, OUT[ch])
            grad = b_inv * (gpre[:, at] - ba[:, at].astype(f32) * factor)
            bst[:, at] = (bg[:, at].astype(f32) + grad).astype(bf16)
            bwd_copy(c2, ch).start()

    def finish_fwd(ch):
        returned(FWD, ch)
        for c2 in range(2):
            for j in range(*OUT[ch]):
                at = cols(c2, j)
                fst[:, at] = (
                    fa[:, at].astype(f32) + route_scale * (f_gate * rows_of(FWD, f_table, (c2, j)))
                ).astype(bf16)
            fwd_copy(c2, ch).start()

    for ch in range(n - 2, n):
        if ch - 2 >= 0:
            finish_fwd(ch - 2)
        give0(FWD, ch)
    for ch in range(max(n - 2, 0), n):
        finish_fwd(ch)

    for copy in give_w:
        copy.wait_send()
    for m in (BWD, FWD):
        for ch in NC:
            for dy, dc in others:
                send_desc(m, ch, dy, dc).wait_send()
                back_desc(m, ch, dy, dc).wait_send()
            for copy in ag_own(m, ch) + [ag_on(m, ch), down3(m, ch), down1(m, ch), up2(m, ch)]:
                copy.wait_send()
        for s in range(4):
            z_copy(m, s).wait_send()
            h_copy(m, s).wait_send()
    for ch in NC:
        for c2 in range(2):
            fwd_copy(c2, ch).wait()
            bwd_copy(c2, ch).wait()


def on_device(
    fwd_act, fwd_ids, bwd_act, bwd_ids, bwd_grad, norm_gain, router, w_gate, w_down, saved_gate
):
    D = fwd_act.shape[1]
    HF = D // 2
    n = len(plan(HF)[0])
    saved = saved_gate[0, 0]
    vmem = pl.BlockSpec(memory_space=pltpu.VMEM)
    hbm = pl.BlockSpec(memory_space=pl.ANY)
    dma = pltpu.SemaphoreType.DMA
    V = pltpu.VMEM
    packs = V((2, 2, EXP, PACK, SUB), bf16)
    sums = V((2, BLK, HF), bf16)
    return pl.pallas_call(
        kernel,
        out_shape=[jax.ShapeDtypeStruct((TOK, D), bf16)] * 2,
        in_specs=[hbm, vmem, hbm, vmem, hbm, vmem, vmem] + [hbm] * 3,
        out_specs=[hbm, hbm],
        scratch_shapes=[
            V((TOK, D), bf16),
            V((TOK, D), bf16),
            V((TOK, D), bf16),
            packs,
            packs,
            V((2, 4, BLK, HF), bf16),
            V((HF, 2 * HS), bf16),
            V((2 * HS, HF), bf16),
            V((2, 4, BLK, HS), f32),
            V((2, 4, BLK, HS), f32),
            V((2, 4, BLK, HS), f32),
            V((2, 4, BLK, 2 * HS), bf16),
            sums, sums, sums, sums, sums, sums, sums,
            packs,
            packs,
            V((TOK, D), bf16),
            V((TOK, D), bf16),
            V((TOK, D), f32),
            V((640, HS), bf16),
            V((4, 8, 256), f32),
            dma((4,)), dma((2,)), dma((2,)), dma((2,)),
            dma((2, n)), dma((2, n, 4, 2)), dma((2, n, 2, 4)),
            dma((2, 3, n)), dma((2, 3, n)),
            dma((2, 4)), dma((2, 4)), dma((2, 4)), dma((2, 4)),
            dma((2, 3, n)), dma((2, 3, n)),
            dma((2, n)), dma((2, n, 4, 2)), dma((2, n, 2, 4)),
            dma((2, 2, n)), dma((2, 2, n)),
        ],
        compiler_params=pltpu.CompilerParams(
            collective_id=0, has_side_effects=True, vmem_limit_bytes=56 * 2**20
        ),
    )(
        fwd_act, fwd_ids.reshape(1, TOK), bwd_act, bwd_ids.reshape(1, TOK), bwd_grad, norm_gain,
        router[0].T, w_gate[0], w_down[0], saved,
    )


def solution(mesh):
    return jax.shard_map(
        on_device,
        mesh=mesh,
        in_specs=(
            P(("pp", "ep"), None),
            P(("pp", "ep"), None),
            P(("pp", "ep"), None),
            P(("pp", "ep"), None),
            P(("pp", "ep"), None),
            P("pp", None),
            P("pp", None, None),
            P(("pp", "ep"), None, None),
            P(("pp", "ep"), None, None),
            P("pp", "ep", None, None),
        ),
        out_specs=(P(("pp", "ep"), None), P(("pp", "ep"), None)),
        check_vma=False,
    )
```

time: 348 us -> 108 us (0.31); the launches traced: 341 us -> 108 us
  waiting for transfers between devices: 232 us -> 0 us
  Pallas kernels: 0 us -> 105 us
  starting transfers between devices: 54.7 us -> 0 us
  local copies, waits for them, and re-layouts: 23.8 us -> 2.64 us
  matrix products: 16.1 us -> 0 us
  other arithmetic: 13.8 us -> 0 us
    all_to_all x5 -> x0, waiting for transfers between devices: 220 us -> none  [the longest x1 62.2 us: on_device(): lax.all_to_all(grad_send, 'ep', split_axis=0, concat_axis=0, tiled=True)]
    pallas_call x0 -> x1, Pallas kernels: none -> 105 us  [on_device(): pl.pallas_call(kernel, out_shape=[jax.ShapeDtypeStruct((TOK, D), bf16)] *...]
    all_to_all x5 -> x0, starting transfers between devices: 44.5 us -> none  [the longest x1 11.5 us: on_device(): lax.all_to_all(grad_send, 'ep', split_axis=0, concat_axis=0, tiled=True)]
    dot_general x8 -> x0, matrix products: 16.1 us -> none  [the longest x1 4.33 us: slice_backward(): jnp.einsum('sch,hd->scd', hidden, down_part, preferred_element_type=jnp.f...]
    ppermute x2 -> x0, waiting for transfers between devices: 12.2 us -> none  [shifted(): lax.ppermute(shard, axis, [(i, (i + by) % peers) for i in range(peers)])]
    ppermute x2 -> x0, starting transfers between devices: 10.2 us -> none  [shifted(): lax.ppermute(shard, axis, [(i, (i + by) % peers) for i in range(peers)])]
    convert_element_type x7 -> x0, local copies, waits for them, and re-layouts: 10.2 us -> none  [the longest x1 4.58 us: slice_forward(): jnp.einsum('sch,hd->scd', hidden, down_part, preferred_element_type=jnp.f...]
    reduce_sum x7 -> x0, other arithmetic: 8.24 us -> none  [the longest x3 7.14 us: fold_slices(): return jnp.sum(wide, axis=1).reshape((-1,) + returned.shape[2:])]
  transfers between devices with their start and end apart: 7 -> 0, of which waited for: 6 -> 0; matrix products, arithmetic and copies ran while one was open for 12% -> 0% of each run, Pallas kernels for 0% -> 0%
where the time goes in v2:
time: 108 us
  Pallas kernels  105 us (97%)
  local copies, waits for them, and re-layouts  2.64 us (2%)
    pallas_call x1, Pallas kernels, on_device(): pl.pallas_call(kernel, out_shape=[jax.ShapeDtypeStruct((TOK, D), bf16)] *...  105 us
    unnamed x4, local copies, waits for them, and re-layouts  2.64 us

profile of v2, /device:TPU:1, one launch (start us, length us, event | category | flops | bytes accessed | tf_op | source)
XLA Modules:
  0.0 108.0 jit_solution(9955837145504426608)
XLA Ops:
  0.6 104.7 %shard_map.113 = (bf16[64,3584]{1,0:T(8,128)(2,1)}, bf16[64,3584]{1,0:T(8,128)(2,1)}) custom-call(bf16[64,3584]{1,0:T(8,128)(2,1)} %fa_hbm.1, s32[1,64]{1,0:T(1,128)} %bitcast.12, bf16[64,3584]{1,0:T(8,128)(2,1)} %ba_hbm.1, s32[1,64]{1,0:T(1,128)} %bitcast.13, bf16[64,3584]{1,0:T(8,128)(2,1)} %bg_hbm.1, bf16[1,3584]{1,0:T(2,128)(2,1)} %gain.1, ...), custom_call_target="tpu_custom_call" | custom-call | tf_op jit(solution)/shard_map/pallas_call | solution.py:535
  105.3 0.0 copy-start
  105.4 1.9 %copy.14 = bf16[64,3584]{1,0:T(8,128)(2,1)} copy(bf16[64,3584]{1,0:T(8,128)(2,1)} %get-tuple-element.4) | data formatting | bytes 917504
  107.2 0.0 copy-done
  107.2 0.8 copy.15
Async XLA Ops:
  105.3 1.9 %copy-start = (bf16[64,3584]{1,0:T(8,128)(2,1)S(1)}, bf16[64,3584]{1,0:T(8,128)(2,1)}, u32[]{:S(2)}) copy-start(bf16[64,3584]{1,0:T(8,128)(2,1)} %get-tuple-element.5) | copy-start | bytes 1376260

commit v3 on v2

--- a/solution.py
+++ b/solution.py
@@ -85,7 +85,7 @@
     d_sib = dev(y, x, 1 - c)
     d_zn = ((pp + 1) % n_pp, ep)
     d_zp = ((pp + n_pp - 1) % n_pp, ep)
-    others = [(dy, dc) for dy in range(4) for dc in range(2) if (dy, dc) != (0, 0)]
+    others = [(2, 0), (2, 1), (1, 0), (3, 0), (1, 1), (3, 1), (0, 1)]
 
     def remote(src, dst, ssem, rsem, device):
         return pltpu.make_async_remote_copy(
@@ -451,14 +451,19 @@
         give0(BWD, ch)
     ready(FWD, 1)
     ready(FWD, 0)
-    mean = jnp.zeros((TOK, SUB), f32)
-    grad_logits = None
-    for ch in NC:
+    def push_fwd(ch):
         give1(FWD, ch)
         if ch + 3 < n:
             give3(FWD, ch + 3)
         if ch + 2 < n:
             give2(FWD, ch + 2)
+
+    half = n // 2
+    mean = jnp.zeros((TOK, SUB), f32)
+    grad_logits = None
+    for ch in NC:
+        if ch % 2 == 0:
+            push_fwd(ch // 2)
         returned(BWD, ch)
         if ch == 0:
             hit = (68 * c + 17 * y).astype(f32) + b_place == iota((TOK, SUB), 1).astype(f32)
@@ -474,8 +479,6 @@
             pre = grad_n * gain[:, cols(*at)].astype(f32)
             gpre[:, cols(*at)] = pre
             mean = mean + pre * ba[:, cols(*at)].astype(f32)
-        if ch >= 2:
-            give0(FWD, ch - 2)
     factor = b_inv * b_inv * (jnp.sum(mean, axis=-1, keepdims=True) * (1.0 / D))
     for ch in NC:
         for c2 in range(2):
@@ -483,6 +486,24 @@
             grad = b_inv * (gpre[:, at] - ba[:, at].astype(f32) * factor)
             bst[:, at] = (bg[:, at].astype(f32) + grad).astype(bf16)
             bwd_copy(c2, ch).start()
+    for ch in range(half, n):
+        push_fwd(ch)
+        give0(FWD, ch - half)
+    for copy in give_w:
+        copy.wait_send()
+    for m in (BWD, FWD):
+        for ch in NC:
+            for dy, dc in others:
+                send_desc(m, ch, dy, dc).wait_send()
+            for copy in ag_own(m, ch) + [ag_on(m, ch), down3(m, ch), up2(m, ch)]:
+                copy.wait_send()
+        for s in range(4):
+            z_copy(m, s).wait_send()
+            h_copy(m, s).wait_send()
+    for ch in NC:
+        for dy, dc in others:
+            back_desc(BWD, ch, dy, dc).wait_send()
+        down1(BWD, ch).wait_send()
 
     def finish_fwd(ch):
         returned(FWD, ch)
@@ -494,25 +515,17 @@
                 ).astype(bf16)
             fwd_copy(c2, ch).start()
 
-    for ch in range(n - 2, n):
-        if ch - 2 >= 0:
-            finish_fwd(ch - 2)
+    for ch in range(n - half, n):
+        if n > 2:
+            finish_fwd(ch - (n - half))
         give0(FWD, ch)
-    for ch in range(max(n - 2, 0), n):
+    for ch in range(half if n > 2 else 0, n):
         finish_fwd(ch)
 
-    for copy in give_w:
-        copy.wait_send()
-    for m in (BWD, FWD):
-        for ch in NC:
-            for dy, dc in others:
-                send_desc(m, ch, dy, dc).wait_send()
-                back_desc(m, ch, dy, dc).wait_send()
-            for copy in ag_own(m, ch) + [ag_on(m, ch), down3(m, ch), down1(m, ch), up2(m, ch)]:
-                copy.wait_send()
-        for s in range(4):
-            z_copy(m, s).wait_send()
-            h_copy(m, s).wait_send()
+    for ch in NC:
+        for dy, dc in others:
+            back_desc(FWD, ch, dy, dc).wait_send()
+        down1(FWD, ch).wait_send()
     for ch in NC:
         for c2 in range(2):
             fwd_copy(c2, ch).wait()

time: 108 us -> 108 us (level)
  no operation moved by 1% of the time
where the time goes in v3:
time: 108 us
  Pallas kernels  105 us (97%)
  local copies, waits for them, and re-layouts  2.64 us (2%)
    pallas_call x1, Pallas kernels, on_device(): pl.pallas_call(kernel, out_shape=[jax.ShapeDtypeStruct((TOK, D), bf16)] *...  105 us
    unnamed x4, local copies, waits for them, and re-layouts  2.64 us

profile of v3, /device:TPU:1, one launch (start us, length us, event | category | flops | bytes accessed | tf_op | source)
XLA Modules:
  0.0 107.9 jit_solution(2555982487260354695)
XLA Ops:
  0.6 104.6 %shard_map.113 = (bf16[64,3584]{1,0:T(8,128)(2,1)}, bf16[64,3584]{1,0:T(8,128)(2,1)}) custom-call(bf16[64,3584]{1,0:T(8,128)(2,1)} %fa_hbm.1, s32[1,64]{1,0:T(1,128)} %bitcast.12, bf16[64,3584]{1,0:T(8,128)(2,1)} %ba_hbm.1, s32[1,64]{1,0:T(1,128)} %bitcast.13, bf16[64,3584]{1,0:T(8,128)(2,1)} %bg_hbm.1, bf16[1,3584]{1,0:T(2,128)(2,1)} %gain.1, ...), custom_call_target="tpu_custom_call" | custom-call | tf_op jit(solution)/shard_map/pallas_call | solution.py:548
  105.3 0.0 copy-start
  105.3 1.9 %copy.14 = bf16[64,3584]{1,0:T(8,128)(2,1)} copy(bf16[64,3584]{1,0:T(8,128)(2,1)} %get-tuple-element.4) | data formatting | bytes 917504
  107.1 0.0 copy-done
  107.2 0.8 copy.15
Async XLA Ops:
  105.3 1.9 %copy-start = (bf16[64,3584]{1,0:T(8,128)(2,1)S(1)}, bf16[64,3584]{1,0:T(8,128)(2,1)}, u32[]{:S(2)}) copy-start(bf16[64,3584]{1,0:T(8,128)(2,1)} %get-tuple-element.5) | copy-start | bytes 1376260
